TPU v7x, 32 devices: a whole 2x2x4 slice. The times are simulated.
32 devices in a mesh: groups: 2 (over y), expert: 4 (over z), fsdp: 4 (over x, core).
Axes of the slice: x: 2, y: 2, z: 4, core: 2. Of those that a mesh axis runs over, the one named last changes fastest.
Arguments:
- tokens: bfloat16 [8192, 2048], P(('groups', 'expert', 'fsdp')), parts along dimension 0, may hold values from -6 to 6
- cotangent: bfloat16 [8192, 2048], P(('groups', 'expert', 'fsdp')), parts along dimension 0, may hold values from -6 to 6
- expert_ids: int32 [8192], P(('groups', 'expert', 'fsdp')), parts along dimension 0, may hold values from 0 to 3, as said below
- gate_weight: bfloat16 [4, 2048, 768], P('expert', 'fsdp'), may hold values from -0.125 to 0.125
- up_weight: bfloat16 [4, 2048, 768], P('expert', 'fsdp'), may hold values from -0.125 to 0.125
- down_weight: bfloat16 [4, 768, 2048], P('expert', None, 'fsdp'), may hold values from -0.21875 to 0.21875
Outputs:
- layer_output: bfloat16 [8192, 2048], P(('groups', 'expert', 'fsdp')), parts along dimension 0
- grad_tokens: bfloat16 [8192, 2048], P(('groups', 'expert', 'fsdp')), parts along dimension 0
- gate_grad: bfloat16 [8, 2048, 768], P(('groups', 'expert'), 'fsdp'), parts along dimension 0
- up_grad: bfloat16 [8, 2048, 768], P(('groups', 'expert'), 'fsdp'), parts along dimension 0
- down_grad: bfloat16 [8, 768, 2048], P(('groups', 'expert'), None, 'fsdp'), parts along dimension 0
There are 2 independent parts, one for each index of `groups`. A program takes and returns all parts, laid end to end along the dimension named above; an argument that names none is the same for every part. Nothing has to cross between parts.
Inputs may be any that keep to these rules, and one draw needn't show every extreme that they name: `expert_ids`: among the 256 tokens of one device (an aligned block of 256), no expert is named more than 128 times; in every draw one expert is named exactly 128 times in every such block.
All inputs are finite; a program needn't handle non-finite values.
Results may differ from a plain program's by a relative error of at most 0.009.
Values may be sent and summed in bfloat16 or wider, within the bound.
A program may use at most 128 MiB of HBM per device.

v0:
```python
import jax
import jax.numpy as jnp
from jax import lax
from jax.sharding import PartitionSpec as P

loss_scale = 0.015625


def slot_positions(expert_ids, expert_count, capacity):
    onehot_table = (
        expert_ids[:, None] == jnp.arange(expert_count, dtype=jnp.int32)[None, :]
    ).astype(jnp.int32)
    earlier = jnp.cumsum(onehot_table, axis=0) - onehot_table
    rank_within = jnp.sum(earlier * onehot_table, axis=1)
    return expert_ids * capacity + rank_within


def contract_last(left, right):
    return lax.dot_general(
        left, right, (((1,), (1,)), ((), ())), preferred_element_type=jnp.float32
    )


def contract_first(left, right):
    return lax.dot_general(
        left, right, (((0,), (0,)), ((), ())), preferred_element_type=jnp.float32
    )


def forward_rows(recv_rows, w_gate, w_up, w_down):
    gate_act = jnp.dot(recv_rows, w_gate, preferred_element_type=jnp.float32)
    up_act = jnp.dot(recv_rows, w_up, preferred_element_type=jnp.float32)
    sigmoid_gate = jax.nn.sigmoid(gate_act)
    hidden = (gate_act * sigmoid_gate * up_act).astype(jnp.bfloat16)
    out_rows = jnp.dot(hidden, w_down, preferred_element_type=jnp.float32).astype(jnp.bfloat16)
    return (gate_act, up_act, hidden, out_rows)


def backward_rows(grad_out, gate_act, up_act, w_gate, w_up, w_down):
    grad_hidden = contract_last(grad_out, w_down)
    sigmoid_gate = jax.nn.sigmoid(gate_act)
    grad_gate = (
        grad_hidden * up_act * sigmoid_gate * (1.0 + gate_act * (1.0 - sigmoid_gate))
    ).astype(jnp.bfloat16)
    grad_up = (grad_hidden * gate_act * sigmoid_gate).astype(jnp.bfloat16)
    grad_rows = (contract_last(grad_gate, w_gate) + contract_last(grad_up, w_up)).astype(
        jnp.bfloat16
    )
    return (grad_gate, grad_up, grad_rows)


def body(tokens, cotangent, expert_ids, gate_weight, up_weight, down_weight):
    tok_rows, feature_count = tokens.shape
    owners = lax.axis_size("expert")
    capacity = 2 * tok_rows // owners
    slot_count = owners * capacity
    slot_of = slot_positions(expert_ids, owners, capacity)
    send_rows = jnp.zeros((slot_count, feature_count), jnp.bfloat16).at[slot_of].set(tokens)
    send_grads = jnp.zeros((slot_count, feature_count), jnp.bfloat16).at[slot_of].set(cotangent)
    full_gate, full_up, full_down = (
        lax.all_gather(gate_weight, "fsdp", axis=1, tiled=True),
        lax.all_gather(up_weight, "fsdp", axis=1, tiled=True),
        lax.all_gather(down_weight, "fsdp", axis=2, tiled=True),
    )
    w_gate, w_up, w_down = (full_gate[0], full_up[0], full_down[0])
    recv_rows, grad_out = (
        lax.all_to_all(send_rows, "expert", split_axis=0, concat_axis=0, tiled=True),
        lax.all_to_all(send_grads, "expert", split_axis=0, concat_axis=0, tiled=True),
    )
    gate_act, up_act, hidden, out_rows = forward_rows(recv_rows, w_gate, w_up, w_down)
    grad_gate, grad_up, grad_rows = backward_rows(grad_out, gate_act, up_act, w_gate, w_up, w_down)
    out_home, grad_home = (
        lax.all_to_all(out_rows, "expert", split_axis=0, concat_axis=0, tiled=True),
        lax.all_to_all(grad_rows, "expert", split_axis=0, concat_axis=0, tiled=True),
    )
    both_grads = jnp.concatenate([grad_gate, grad_up], axis=1)
    first_terms = contract_first(recv_rows, both_grads)
    second_terms = contract_first(grad_out, hidden)
    summed = lax.psum_scatter(
        (jnp.concatenate([first_terms, second_terms], axis=1) * loss_scale).astype(jnp.bfloat16),
        "fsdp",
        scatter_dimension=0,
        tiled=True,
    )
    hidden_size = w_gate.shape[1]
    gate_grad = summed[:, :hidden_size][None]
    up_grad = summed[:, hidden_size : 2 * hidden_size][None]
    down_grad = jnp.transpose(summed[:, 2 * hidden_size :])[None]
    layer_output = out_home[slot_of]
    grad_tokens = grad_home[slot_of]
    return (layer_output, grad_tokens, gate_grad, up_grad, down_grad)


def solution(mesh):
    placed = (
        P(("groups", "expert", "fsdp"), None),
        P(("groups", "expert", "fsdp"), None),
        P(("groups", "expert", "fsdp")),
        P("expert", "fsdp", None),
        P("expert", "fsdp", None),
        P("expert", None, "fsdp"),
    )
    return jax.shard_map(
        body,
        mesh=mesh,
        in_specs=placed,
        out_specs=(
            P(("groups", "expert", "fsdp"), None),
            P(("groups", "expert", "fsdp"), None),
            P(("groups", "expert"), "fsdp", None),
            P(("groups", "expert"), "fsdp", None),
            P(("groups", "expert"), None, "fsdp"),
        ),
        check_vma=False,
    )
```

profile of v0, /device:TPU:0, one launch (start us, length us, event | category | flops | bytes accessed | tf_op | source)
XLA Modules:
  0.0 271.1 jit_solution(12203110211342138155)
XLA Ops:
  7.2 0.0 all-gather.6.cloned.1.call-start
  7.2 0.7 all-gather.6.cloned.1.call-update
  7.9 0.0 all-gather.8.cloned.1.call-start
  7.9 0.7 all-gather.8.cloned.1.call-update
  8.6 0.7 compare_convert_fusion
  9.3 1.2 reduce-window.6
  10.5 0.1 slice.24
  10.6 0.1 copy.15
  10.8 0.1 copy.16
  10.9 0.1 add_bitcast_fusion
  10.9 0.7 fusion.28
  11.6 0.7 compare_select_fusion
  12.3 4.4 %scatter_custom_fusion = bf16[512,2048]{1,0:T(8,128)(2,1)} fusion(s32[256]{0:T(256)S(1)} %compare_select_fusion, bf16[256,2048]{1,0:T(8,128)(2,1)} %param.6, bf16[]{:T(256)} %constant.6.clone.1), kind=kCustom, calls=%fused_computation.30 | custom fusion | bytes 2097664 | tf_op jit(solution)/shard_map/scatter | solution.py:58
  16.7 6.3 %all-to-all-start = ((bf16[4,128,2048]{2,1,0:T(8,128)(2,1)}), bf16[4,128,2048]{2,1,0:T(8,128)(2,1)S(1)}, u32[]{:S(2)}, u32[]{:S(2)}) async-start(bf16[4,128,2048]{2,1,0:T(8,128)(2,1)} %bitcast.3), calls=%async_computation | async-start | bytes 4194304 | tf_op jit(solution)/shard_map/all_to_all | solution.py:67
  23.0 0.0 all-gather.4.cloned.1.call-start
  23.1 0.7 all-gather.4.cloned.1.call-update
  23.8 4.4 %scatter_custom_fusion.1 = bf16[512,2048]{1,0:T(8,128)(2,1)} fusion(s32[256]{0:T(256)S(1)} %compare_select_fusion, bf16[256,2048]{1,0:T(8,128)(2,1)} %param.7, bf16[]{:T(256)} %constant.6.clone.1), kind=kCustom, calls=%fused_computation.28 | custom fusion | bytes 2097664 | tf_op jit(solution)/shard_map/scatter | solution.py:59
  28.2 43.1 %all-to-all-done = bf16[4,128,2048]{2,1,0:T(8,128)(2,1)S(1)} async-done(((bf16[4,128,2048]{2,1,0:T(8,128)(2,1)}), bf16[4,128,2048]{2,1,0:T(8,128)(2,1)S(1)}, u32[]{:S(2)}, u32[]{:S(2)}) %all-to-all-start) | async-done | bytes 2097184 | tf_op jit(solution)/shard_map/all_to_all | solution.py:67
  71.2 0.0 copy-start
  71.2 1.3 copy-done
  72.6 3.6 %all-to-all-start.2 = ((bf16[4,128,2048]{2,1,0:T(8,128)(2,1)}), bf16[4,128,2048]{2,1,0:T(8,128)(2,1)S(1)}, u32[]{:S(2)}, u32[]{:S(2)}) async-start(bf16[4,128,2048]{2,1,0:T(8,128)(2,1)} %bitcast.71), calls=%async_computation.2 | async-start | bytes 4194304 | tf_op jit(solution)/shard_map/all_to_all | solution.py:68
  76.2 0.2 reduce-scatter.2.cloned.1.call-start
  76.4 0.0 all-gather.6.cloned.1.call-done
  76.4 5.6 %fusion.7 = f32[512,768]{1,0:T(8,128)} fusion(bf16[512,2048]{1,0:T(8,128)(2,1)} %bitcast.72, bf16[1,2048,768]{2,1,0:T(8,128)(2,1)} %all-gather.6.cloned.1.call-done), kind=kOutput, calls=%fused_computation.13 | convolution fusion | flops 1610612736 | bytes 6815744 | tf_op jit(solution)/shard_map/dot_general | solution.py:32
  82.1 41.8 %all-to-all-done.2 = bf16[4,128,2048]{2,1,0:T(8,128)(2,1)S(1)} async-done(((bf16[4,128,2048]{2,1,0:T(8,128)(2,1)}), bf16[4,128,2048]{2,1,0:T(8,128)(2,1)S(1)}, u32[]{:S(2)}, u32[]{:S(2)}) %all-to-all-start.2) | async-done | bytes 2097184 | tf_op jit(solution)/shard_map/all_to_all | solution.py:68
  123.9 0.0 all-gather.8.cloned.1.call-done
  123.9 4.9 %fusion.1 = f32[512,768]{1,0:T(8,128)} fusion(bf16[512,2048]{1,0:T(8,128)(2,1)S(1)} %bitcast.69, bf16[1,768,2048]{2,1,0:T(8,128)(2,1)} %all-gather.8.cloned.1.call-done), kind=kOutput, calls=%fused_computation.7 | convolution fusion | flops 1610612736 | bytes 6815744 | tf_op jit(solution)/shard_map/dot_general | solution.py:19
  128.7 0.0 all-gather.4.cloned.1.call-done
  128.7 5.7 %multiply_convert_fusion.1 = (bf16[512,768]{1,0:T(8,128)(2,1)S(1)}, bf16[512,768]{1,0:T(8,128)(2,1)S(1)}, bf16[512,768]{1,0:T(8,128)(2,1)S(1)}) fusion(f32[512,768]{1,0:T(8,128)} %fusion.1, f32[512,768]{1,0:T(8,128)} %fusion.7, bf16[512,2048]{1,0:T(8,128)(2,1)} %bitcast.73, bf16[1,2048,768]{2,1,0:T(8,128)(2,1)} %all-gather.4.cloned.1.call-done), kind=kOutput, calls=%fused_computation.25 | convolution fusion | flops 1616904192 | bytes 10747904 | tf_op jit(solution)/shard_map/dot_general | solution.py:31
  134.5 0.0 copy-start.3
  134.5 0.0 copy-start.5
  134.5 0.0 copy-start.1
  134.5 1.9 fusion.30
  136.4 0.0 copy-done.3
  136.4 0.0 copy-done.5
  136.4 0.2 copy-done.1
  136.7 3.6 %fusion.18 = f32[2048,1536]{0,1:T(8,128)S(1)} fusion(bf16[512,2048]{1,0:T(8,128)(2,1)S(1)} %bitcast.74, bf16[512,768]{1,0:T(8,128)(2,1)S(1)} %get-tuple-element.17, bf16[512,768]{1,0:T(8,128)(2,1)S(1)} %get-tuple-element.15), kind=kOutput, calls=%fused_computation.20 | convolution fusion | flops 3224371200 | bytes 16252928 | tf_op jit(solution)/shard_map/dot_general | solution.py:25
  140.3 5.6 %fusion = bf16[2048,2304]{0,1:T(8,128)(2,1)} fusion(f32[2048,768]{0,1:T(8,128)S(1)} %fusion.30, f32[2048,1536]{0,1:T(8,128)S(1)} %fusion.18), kind=kLoop, calls=%fused_computation.5 | loop fusion | flops 14155776 | bytes 28311552 | tf_op jit(solution)/shard_map/convert_element_type | solution.py:80
  145.9 0.0 reduce-scatter.2.cloned.1.call-update
  145.9 5.1 %fusion.13 = bf16[512,2048]{1,0:T(8,128)(2,1)} fusion(bf16[512,768]{1,0:T(8,128)(2,1)S(1)} %get-tuple-element.16, bf16[1,768,2048]{2,1,0:T(8,128)(2,1)} %all-gather.8.cloned.1.call-done), kind=kOutput, calls=%fused_computation.19 | convolution fusion | flops 1611661312 | bytes 6029312 | tf_op jit(solution)/shard_map/dot_general | solution.py:35
  151.0 3.8 %all-to-all-start.1 = ((bf16[4,128,2048]{2,1,0:T(8,128)(2,1)}), bf16[4,128,2048]{2,1,0:T(8,128)(2,1)S(1)}, u32[]{:S(2)}, u32[]{:S(2)}) async-start(bf16[4,128,2048]{2,1,0:T(8,128)(2,1)} %bitcast.76), calls=%async_computation.1 | async-start | bytes 4194304 | tf_op jit(solution)/shard_map/all_to_all | solution.py:73
  154.7 0.0 copy-start.2
  154.7 0.0 copy-start.4
  154.8 5.1 %fusion.5 = f32[512,2048]{1,0:T(8,128)S(1)} fusion(bf16[512,768]{1,0:T(8,128)(2,1)} %copy-done.5, bf16[1,2048,768]{2,1,0:T(8,128)(2,1)} %all-gather.6.cloned.1.call-done), kind=kOutput, calls=%fused_computation.11 | convolution fusion | flops 1610612736 | bytes 8126464 | tf_op jit(solution)/shard_map/dot_general | solution.py:19
  159.9 0.0 copy-done.2
  159.9 0.1 copy-done.4
  160.0 3.2 %add_convert_fusion = bf16[512,2048]{1,0:T(8,128)(2,1)} fusion(f32[512,2048]{1,0:T(8,128)S(1)} %fusion.5, bf16[512,768]{1,0:T(8,128)(2,1)S(1)} %copy-done.4, bf16[1,2048,768]{2,1,0:T(8,128)(2,1)S(1)} %copy-done.2), kind=kOutput, calls=%fused_computation.6 | convolution fusion | flops 1612709888 | bytes 10223616 | tf_op jit(solution)/shard_map/dot_general | solution.py:19
  163.1 39.0 %all-to-all-done.1 = bf16[4,128,2048]{2,1,0:T(8,128)(2,1)S(1)} async-done(((bf16[4,128,2048]{2,1,0:T(8,128)(2,1)}), bf16[4,128,2048]{2,1,0:T(8,128)(2,1)S(1)}, u32[]{:S(2)}, u32[]{:S(2)}) %all-to-all-start.1) | async-done | bytes 2097184 | tf_op jit(solution)/shard_map/all_to_all | solution.py:73
  202.2 4.5 %all-to-all-start.3 = ((bf16[4,128,2048]{2,1,0:T(8,128)(2,1)}), bf16[4,128,2048]{2,1,0:T(8,128)(2,1)}, u32[]{:S(2)}, u32[]{:S(2)}) async-start(bf16[4,128,2048]{2,1,0:T(8,128)(2,1)} %bitcast.75), calls=%async_computation.3 | async-start | bytes 4194304 | tf_op jit(solution)/shard_map/all_to_all | solution.py:74
  206.7 2.3 gather_fusion
  209.0 45.4 %all-to-all-done.3 = bf16[4,128,2048]{2,1,0:T(8,128)(2,1)} async-done(((bf16[4,128,2048]{2,1,0:T(8,128)(2,1)}), bf16[4,128,2048]{2,1,0:T(8,128)(2,1)}, u32[]{:S(2)}, u32[]{:S(2)}) %all-to-all-start.3) | async-done | bytes 2097184 | tf_op jit(solution)/shard_map/all_to_all | solution.py:74
  254.4 5.2 %gather_fusion.1 = bf16[256,2048]{1,0:T(8,128)(2,1)} fusion(bf16[512,2048]{1,0:T(8,128)(2,1)} %bitcast.13, s32[1024]{0:T(1024)S(1)} %pad_clamp_fusion), kind=kCustom, calls=%fused_computation.1 | custom fusion | bytes 2098176 | tf_op jit(solution)/shard_map/gather | solution.py:90
  259.6 0.0 reduce-scatter.2.cloned.1.call-done
  259.6 2.6 slice_bitcast_fusion
  262.2 1.2 copy.18
  263.4 1.2 copy.17
  (3 shorter events, 0.0 us)
Async XLA Ops:
  7.2 69.3 %all-gather.6.cloned.1.call-start = ((), (), s32[]{:S(2)}) async-start(), calls=%async_computation.6 | async-start | bytes 3932160 | tf_op jit(solution)/shard_map/all_gather | solution.py:62
  7.9 116.0 %all-gather.8.cloned.1.call-start = ((), (), s32[]{:S(2)}) async-start(), calls=%async_computation.7 | async-start | bytes 3932160 | tf_op jit(solution)/shard_map/all_gather | solution.py:63
  16.7 54.5 %all-to-all-start = ((bf16[4,128,2048]{2,1,0:T(8,128)(2,1)}), bf16[4,128,2048]{2,1,0:T(8,128)(2,1)S(1)}, u32[]{:S(2)}, u32[]{:S(2)}) async-start(bf16[4,128,2048]{2,1,0:T(8,128)(2,1)} %bitcast.3), calls=%async_computation | async-start | bytes 4194304 | tf_op jit(solution)/shard_map/all_to_all | solution.py:67
  23.0 105.7 %all-gather.4.cloned.1.call-start = ((), (), s32[]{:S(2)}) async-start(), calls=%async_computation.5 | async-start | bytes 3932160 | tf_op jit(solution)/shard_map/all_gather | solution.py:61
  71.2 1.3 copy-start
  72.6 51.3 %all-to-all-start.2 = ((bf16[4,128,2048]{2,1,0:T(8,128)(2,1)}), bf16[4,128,2048]{2,1,0:T(8,128)(2,1)S(1)}, u32[]{:S(2)}, u32[]{:S(2)}) async-start(bf16[4,128,2048]{2,1,0:T(8,128)(2,1)} %bitcast.71), calls=%async_computation.2 | async-start | bytes 4194304 | tf_op jit(solution)/shard_map/all_to_all | solution.py:68
  76.2 183.4 %reduce-scatter.2.cloned.1.call-start = ((), (), s32[]{:S(2)}) async-start(), calls=%async_computation.8 | async-start | bytes 11796480 | tf_op jit(solution)/shard_map/reduce_scatter | solution.py:79
  134.5 1.9 copy-start.3
  134.5 1.9 copy-start.5
  134.5 2.2 copy-start.1
  151.0 51.2 %all-to-all-start.1 = ((bf16[4,128,2048]{2,1,0:T(8,128)(2,1)}), bf16[4,128,2048]{2,1,0:T(8,128)(2,1)S(1)}, u32[]{:S(2)}, u32[]{:S(2)}) async-start(bf16[4,128,2048]{2,1,0:T(8,128)(2,1)} %bitcast.76), calls=%async_computation.1 | async-start | bytes 4194304 | tf_op jit(solution)/shard_map/all_to_all | solution.py:73
  154.7 5.2 %copy-start.2 = (bf16[1,2048,768]{2,1,0:T(8,128)(2,1)S(1)}, bf16[1,2048,768]{2,1,0:T(8,128)(2,1)}, u32[]{:S(2)}) copy-start(bf16[1,2048,768]{2,1,0:T(8,128)(2,1)} %all-gather.4.cloned.1.call-done) | copy-start | bytes 9437188
  154.7 5.2 %copy-start.4 = (bf16[512,768]{1,0:T(8,128)(2,1)S(1)}, bf16[512,768]{1,0:T(8,128)(2,1)}, u32[]{:S(2)}) copy-start(bf16[512,768]{1,0:T(8,128)(2,1)} %copy-done.3) | copy-start | bytes 2359300
  202.2 52.2 %all-to-all-start.3 = ((bf16[4,128,2048]{2,1,0:T(8,128)(2,1)}), bf16[4,128,2048]{2,1,0:T(8,128)(2,1)}, u32[]{:S(2)}, u32[]{:S(2)}) async-start(bf16[4,128,2048]{2,1,0:T(8,128)(2,1)} %bitcast.75), calls=%async_computation.3 | async-start | bytes 4194304 | tf_op jit(solution)/shard_map/all_to_all | solution.py:74
Sparse Core Ops, SparseCore 0:
  9.6 31.2 all-gather.5
  42.4 28.5 all-gather.7
  72.6 28.5 all-gather.3
  146.0 77.5 reduce-scatter.1
where the time goes:
time: 272 us; the launch traced here: 271 us
  waiting for transfers between devices  171 us (63%)
  matrix products  35.1 us (13%)
  local copies, waits for them, and re-layouts  23.2 us (9%)
  starting transfers between devices  18.5 us (7%)
  between operations  13.9 us (5%)
  other arithmetic  8.99 us (3%)
    all_to_all x1, waiting for transfers between devices, body(): lax.all_to_all(grad_rows, 'expert', split_axis=0, concat_axis=0, tiled=True)  45.4 us
    all_to_all x1, waiting for transfers between devices, body(): lax.all_to_all(send_rows, 'expert', split_axis=0, concat_axis=0, tiled=True)  43.1 us
    all_to_all x1, waiting for transfers between devices, body(): lax.all_to_all(send_grads, 'expert', split_axis=0, concat_axis=0, tiled=T...  41.8 us
    all_to_all x1, waiting for transfers between devices, body(): lax.all_to_all(out_rows, 'expert', split_axis=0, concat_axis=0, tiled=True)  39 us
    dot_general x3, matrix products, contract_last(): lax.dot_general(left, right, (((1,), (1,)), ((), ())), preferred_element_...  13.2 us
    all_to_all x1, starting transfers between devices, body(): lax.all_to_all(send_rows, 'expert', split_axis=0, concat_axis=0, tiled=True)  6.32 us
    dot_general x1, matrix products, forward_rows(): gate_act = jnp.dot(recv_rows, w_gate, preferred_element_type=jnp.float32)  5.74 us
    dot_general x1, matrix products, forward_rows(): up_act = jnp.dot(recv_rows, w_up, preferred_element_type=jnp.float32)  5.63 us
  transfers between devices with their start and end apart: 8, of which 4 were waited for; matrix products, arithmetic and copies ran while one was open for 16% of the time, Pallas kernels for 0%

commit v1 on v0

v1 whole, which is shorter than its diff:
```python
import jax
import jax.numpy as jnp
from jax import lax
from jax.sharding import PartitionSpec as P

loss_scale = 0.015625
bf16 = jnp.bfloat16
f32 = jnp.float32


def dot_dims(left, right, l, r):
    return lax.dot_general(left, right, (((l,), (r,)), ((), ())), preferred_element_type=f32)


def shift(x, axis, k):
    n = lax.axis_size(axis)
    return lax.ppermute(x, axis, [(i, (i + k) % n) for i in range(n)])


def swap_core(x):
    n = lax.axis_size("fsdp")
    return lax.ppermute(x, "fsdp", [(i, i ^ 1) for i in range(n)])


def gather_weight(w, dim):
    n = lax.axis_size("fsdp")
    me = lax.axis_index("fsdp")
    core = me % 2
    size = w.shape[dim]
    shape = list(w.shape)
    shape[dim] = size * n
    full = jnp.zeros(shape, w.dtype)
    for j in range(n // 2):
        mine = w if j == 0 else shift(w, "fsdp", 2 * j)
        other = swap_core(mine)
        owner = (me - 2 * j + n) % n
        full = lax.dynamic_update_slice_in_dim(full, mine, owner * size, dim)
        full = lax.dynamic_update_slice_in_dim(full, other, (owner + 1 - 2 * core) * size, dim)
    return full


def scatter_sum(part):
    n = lax.axis_size("fsdp")
    me = lax.axis_index("fsdp")
    core = me % 2
    cols = part.shape[1]
    blocks = part.reshape(n // 2, 2, part.shape[0] // n, cols)
    keep = lax.dynamic_index_in_dim(blocks, core, 1, keepdims=False)
    give = lax.dynamic_index_in_dim(blocks, 1 - core, 1, keepdims=False)
    chip = keep.astype(f32) + swap_core(give).astype(f32)
    x = me // 2
    half = n // 2
    total = lax.dynamic_index_in_dim(chip, x, 0, keepdims=False)
    chip16 = chip.astype(bf16)
    for j in range(1, half):
        out = lax.dynamic_index_in_dim(chip16, (x + j) % half, 0, keepdims=False)
        total = total + shift(out, "fsdp", 2 * j).astype(f32)
    return total.astype(bf16)


def body(tokens, cotangent, expert_ids, gate_weight, up_weight, down_weight):
    rows, features = tokens.shape
    owners = lax.axis_size("expert")
    me = lax.axis_index("expert")
    cap = 2 * rows // owners
    w_gate = gather_weight(gate_weight[0], 0)
    w_up = gather_weight(up_weight[0], 0)
    w_down = gather_weight(down_weight[0], 1)
    onehot = (expert_ids[:, None] == jnp.arange(owners, dtype=jnp.int32)[None, :]).astype(bf16)
    t = jnp.arange(rows, dtype=jnp.int32)
    before = (t[None, :] < t[:, None]).astype(bf16)
    earlier = jnp.dot(before, onehot, preferred_element_type=f32)
    rank = jnp.sum(earlier * onehot.astype(f32), axis=1).astype(jnp.int32)
    slot = ((expert_ids - me + owners) % owners) * cap + rank
    order = [k for k in range(owners) if k % 2 == 0] + [k for k in range(owners) if k % 2]
    half = owners // 2
    chunks = (order[:half], order[half:])

    def select(ks):
        want = jnp.concatenate([k * cap + jnp.arange(cap, dtype=jnp.int32) for k in ks])
        return (want[:, None] == slot[None, :]).astype(bf16)

    picks = [select(ks) for ks in chunks]
    recv = []
    for ks, pick in zip(chunks, picks):
        got = []
        for array in (tokens, cotangent):
            sent = jnp.dot(pick, array, preferred_element_type=f32).astype(bf16)
            got.append(
                jnp.concatenate(
                    [
                        sent[i * cap : (i + 1) * cap]
                        if k == 0
                        else shift(sent[i * cap : (i + 1) * cap], "expert", k)
                        for i, k in enumerate(ks)
                    ]
                )
            )
        recv.append(got)
    hiddens, gates, ups = [], [], []
    home_out, home_grad = [], []
    for ks, (x, g) in zip(chunks, recv):
        gate_act = jnp.dot(x, w_gate, preferred_element_type=f32)
        up_act = jnp.dot(x, w_up, preferred_element_type=f32)
        s = jax.nn.sigmoid(gate_act)
        hidden = (gate_act * s * up_act).astype(bf16)
        out = jnp.dot(hidden, w_down, preferred_element_type=f32).astype(bf16)
        grad_hidden = dot_dims(g, w_down, 1, 1)
        grad_gate = (grad_hidden * up_act * s * (1.0 + gate_act * (1.0 - s))).astype(bf16)
        grad_up = (grad_hidden * gate_act * s).astype(bf16)
        grad = (dot_dims(grad_gate, w_gate, 1, 1) + dot_dims(grad_up, w_up, 1, 1)).astype(bf16)
        hiddens.append(hidden)
        gates.append(grad_gate)
        ups.append(grad_up)
        for result, home in ((out, home_out), (grad, home_grad)):
            home.extend(
                result[i * cap : (i + 1) * cap]
                if k == 0
                else shift(result[i * cap : (i + 1) * cap], "expert", -k)
                for i, k in enumerate(ks)
            )
    x_all = jnp.concatenate([recv[0][0], recv[1][0]])
    g_all = jnp.concatenate([recv[0][1], recv[1][1]])
    gate_part = (dot_dims(x_all, jnp.concatenate(gates), 0, 0) * loss_scale).astype(bf16)
    up_part = (dot_dims(x_all, jnp.concatenate(ups), 0, 0) * loss_scale).astype(bf16)
    down_part = (dot_dims(g_all, jnp.concatenate(hiddens), 0, 0) * loss_scale).astype(bf16)
    gate_grad = scatter_sum(gate_part)[None]
    up_grad = scatter_sum(up_part)[None]
    down_grad = jnp.transpose(scatter_sum(down_part))[None]
    pick_all = jnp.concatenate(picks)
    layer_output = dot_dims(pick_all, jnp.concatenate(home_out), 0, 0).astype(bf16)
    grad_tokens = dot_dims(pick_all, jnp.concatenate(home_grad), 0, 0).astype(bf16)
    return (layer_output, grad_tokens, gate_grad, up_grad, down_grad)


def solution(mesh):
    rows = P(("groups", "expert", "fsdp"), None)
    return jax.shard_map(
        body,
        mesh=mesh,
        in_specs=(
            rows,
            rows,
            P(("groups", "expert", "fsdp")),
            P("expert", "fsdp", None),
            P("expert", "fsdp", None),
            P("expert", None, "fsdp"),
        ),
        out_specs=(
            rows,
            rows,
            P(("groups", "expert"), "fsdp", None),
            P(("groups", "expert"), "fsdp", None),
            P(("groups", "expert"), None, "fsdp"),
        ),
        check_vma=False,
    )
```

time: 272 us -> 236 us (0.87)
  the two profiles are of different devices: /device:TPU:0 before, /device:TPU:21 now
where the time goes in v1:
time: 236 us; the launch traced here: 233 us
  waiting for transfers between devices  123 us (52%)
  starting transfers between devices  34.1 us (14%)
  local copies, waits for them, and re-layouts  33.9 us (14%)
  matrix products  30.6 us (13%)
  other arithmetic  9.24 us (4%)
    ppermute x18, waiting for transfers between devices, shift(): return lax.ppermute(x, axis, [(i, (i + k) % n) for i in range(n)])  123 us
    dot_general x11, matrix products, dot_dims(): lax.dot_general(left, right, (((l,), (r,)), ((), ())), preferred_element_...  19.2 us
    ppermute x18, starting transfers between devices, shift(): return lax.ppermute(x, axis, [(i, (i + k) % n) for i in range(n)])  17.7 us
    ppermute x9, starting transfers between devices, swap_core(): return lax.ppermute(x, 'fsdp', [(i, i ^ 1) for i in range(n)])  16.4 us
    dynamic_update_slice x6, local copies, waits for them, and re-layouts, gather_weight(): full = lax.dynamic_update_slice_in_dim(full, mine, owner * size, dim)  8.77 us
    slice x4, local copies, waits for them, and re-layouts, body(): sent[i * cap:(i + 1) * cap]  5.58 us
  transfers between devices with their start and end apart: 27, of which 9 were waited for; matrix products, arithmetic and copies ran while one was open for 30% of the time, Pallas kernels for 0%

profile of v1, /device:TPU:21, one launch (start us, length us, event | category | flops | bytes accessed | tf_op | source)
XLA Modules:
  0.0 232.6 jit_solution(11584837703841926198)
XLA Ops:
  1.4 1.2 collective-permute-start.8
  4.3 1.7 convolution_convert_fusion.4
  6.0 1.1 fusion.86
  7.1 1.3 collective-permute-start.11
  8.8 1.4 convolution_convert_fusion.2
  11.3 2.3 fusion.82
  13.5 1.1 fusion.80
  14.6 1.1 fusion.84
  16.1 1.2 constant_dynamic-update-slice_fusion.5
  17.6 1.5 copy-done.8
  19.1 1.2 constant_dynamic-update-slice_fusion.9
  20.5 1.8 constant_dynamic-update-slice_fusion.13
  22.3 10.7 %collective-permute-start.4 = (bf16[512,768]{1,0:T(8,128)(2,1)}, bf16[512,768]{1,0:T(8,128)(2,1)}, u32[]{:S(2)}, u32[]{:S(2)}) collective-permute-start(bf16[512,768]{1,0:T(8,128)(2,1)} %bitcast.1), channel_id=1, source_target_pairs={{0,1},{1,0},{2,3},{3,2},{4,5},{5,4},{6,7},{7,6},{8,9},{9,8},{10,11... | collective-permute-start | bytes 2359304 | tf_op jit(solution)/shard_map/ppermute | solution.py:22
  33.9 1.3 constant_dynamic-update-slice_fusion.1
  35.1 1.1 constant_dynamic-update-slice_fusion
  36.5 1.1 collective-permute-done.5
  37.7 1.3 collective-permute-start.6
  39.0 2.1 constant_dynamic-update-slice_fusion.4
  41.1 2.1 constant_dynamic-update-slice_fusion.3
  43.5 11.0 %collective-permute-done.2 = bf16[512,768]{1,0:T(8,128)(2,1)} collective-permute-done((bf16[512,768]{1,0:T(8,128)(2,1)}, bf16[512,768]{1,0:T(8,128)(2,1)}, u32[]{:S(2)}, u32[]{:S(2)}) %collective-permute-start.2) | collective-permute-done | bytes 786464 | tf_op jit(solution)/shard_map/ppermute | solution.py:17
  55.4 1.2 constant_dynamic-update-slice_fusion.8
  56.6 1.3 constant_dynamic-update-slice_fusion.7
  57.9 1.3 collective-permute-start.17
  59.3 1.2 constant_dynamic-update-slice_fusion.11
  60.8 2.4 %collective-permute-start = (bf16[128,2048]{1,0:T(8,128)(2,1)S(1)}, bf16[128,2048]{1,0:T(8,128)(2,1)S(1)}, u32[]{:S(2)}, u32[]{:S(2)}) collective-permute-start(bf16[128,2048]{1,0:T(8,128)(2,1)S(1)} %copy-done.12), channel_id=1, source_target_pairs={{0,8},{4,12},{8,0},{12,4},{1,9},{5,13},{9,1},{13,5},{2,10},{6,14},... | collective-permute-start | bytes 1572872 | tf_op jit(solution)/shard_map/ppermute | solution.py:17
  63.3 1.0 fusion.87
  64.3 7.3 %collective-permute-done.17 = bf16[128,2048]{1,0:T(8,128)(2,1)S(1)} collective-permute-done((bf16[128,2048]{1,0:T(8,128)(2,1)S(1)}, bf16[128,2048]{1,0:T(8,128)(2,1)S(1)}, u32[]{:S(2)}, u32[]{:S(2)}) %collective-permute-start.17) | collective-permute-done | bytes 524320 | tf_op jit(solution)/shard_map/ppermute | solution.py:17
  71.6 1.0 fusion.31
  72.6 1.2 multiply_convert_fusion.4
  73.8 1.0 convolution_convert_fusion.6
  74.9 1.2 collective-permute-start.14
  76.4 39.1 %collective-permute-done.15 = bf16[128,2048]{1,0:T(8,128)(2,1)S(1)} collective-permute-done((bf16[128,2048]{1,0:T(8,128)(2,1)S(1)}, bf16[128,2048]{1,0:T(8,128)(2,1)S(1)}, u32[]{:S(2)}, u32[]{:S(2)}) %collective-permute-start.15) | collective-permute-done | bytes 524320 | tf_op jit(solution)/shard_map/ppermute | solution.py:17
  115.6 1.0 fusion.27
  116.6 10.2 %collective-permute-done = bf16[128,2048]{1,0:T(8,128)(2,1)S(1)} collective-permute-done((bf16[128,2048]{1,0:T(8,128)(2,1)S(1)}, bf16[128,2048]{1,0:T(8,128)(2,1)S(1)}, u32[]{:S(2)}, u32[]{:S(2)}) %collective-permute-start) | collective-permute-done | bytes 524320 | tf_op jit(solution)/shard_map/ppermute | solution.py:17
  127.8 1.2 multiply_convert_fusion.6
  129.0 1.0 convolution_convert_fusion.7
  130.1 3.2 %collective-permute-start.10 = (bf16[128,2048]{1,0:T(8,128)(2,1)S(1)}, bf16[128,2048]{1,0:T(8,128)(2,1)S(1)}, u32[]{:S(2)}, u32[]{:S(2)}) collective-permute-start(bf16[128,2048]{1,0:T(8,128)(2,1)S(1)} %get-tuple-element.20), channel_id=1, source_target_pairs={{0,8},{4,12},{8,0},{12,4},{1,9},{5,13},{9,1},{13,5},{2,10},{6,14},... | collective-permute-start | bytes 1572872 | tf_op jit(solution)/shard_map/ppermute | solution.py:17
  133.3 1.0 fusion.89
  134.3 1.0 fusion.1
  135.3 1.1 fusion.81
  136.4 3.0 %multiply_convert_fusion.2 = bf16[2048,768]{1,0:T(8,128)(2,1)S(1)} fusion(bf16[256,768]{1,0:T(8,128)(2,1)S(1)} %get-tuple-element.8, bf16[256,768]{1,0:T(8,128)(2,1)S(1)} %get-tuple-element.5, bf16[128,2048]{1,0:T(8,128)(2,1)} %collective-permute-done.12, bf16[128,2048]{1,0:T(8,128)(2,1)} %collective-permute-done.11, ...), kind=kOutput, calls=%fused_computation.2 | convolution fusion | flops 1623719936 | bytes 6029312 | tf_op jit(solution)/shard_map/dot_general | solution.py:12
  140.4 3.0 %multiply_convert_fusion.1 = bf16[2048,768]{1,0:T(8,128)(2,1)S(1)} fusion(bf16[256,768]{1,0:T(8,128)(2,1)S(1)} %get-tuple-element.10, bf16[256,768]{1,0:T(8,128)(2,1)S(1)} %get-tuple-element.7, bf16[128,2048]{1,0:T(8,128)(2,1)} %collective-permute-done.12, bf16[128,2048]{1,0:T(8,128)(2,1)} %collective-permute-done.11, ...), kind=kOutput, calls=%fused_computation.1 | convolution fusion | flops 1623719936 | bytes 6029312 | tf_op jit(solution)/shard_map/dot_general | solution.py:12
  143.7 2.1 multiply_convert_fusion
  145.8 1.0 fusion.88
  146.8 1.0 fusion
  148.0 2.2 collective-permute-done.14
  150.2 1.2 collective-permute-start.25
  151.3 1.1 fusion.79
  152.4 19.3 %collective-permute-done.10 = bf16[128,2048]{1,0:T(8,128)(2,1)S(1)} collective-permute-done((bf16[128,2048]{1,0:T(8,128)(2,1)S(1)}, bf16[128,2048]{1,0:T(8,128)(2,1)S(1)}, u32[]{:S(2)}, u32[]{:S(2)}) %collective-permute-start.10) | collective-permute-done | bytes 524320 | tf_op jit(solution)/shard_map/ppermute | solution.py:17
  171.8 1.7 convolution_convert_fusion.1
  173.5 3.1 %collective-permute-start.16 = (bf16[128,2048]{1,0:T(8,128)(2,1)}, bf16[128,2048]{1,0:T(8,128)(2,1)}, u32[]{:S(2)}, u32[]{:S(2)}) collective-permute-start(bf16[128,2048]{1,0:T(8,128)(2,1)} %get-tuple-element.12), channel_id=1, source_target_pairs={{0,8},{4,12},{8,0},{12,4},{1,9},{5,13},{9,1},{13,5},{2,10},{6,14},... | collective-permute-start | bytes 1572872 | tf_op jit(solution)/shard_map/ppermute | solution.py:17
  177.0 1.1 fusion.38
  178.0 1.2 collective-permute-start.22
  179.6 1.1 fusion.39
  182.5 2.3 copy.12
  184.8 1.0 collective-permute-start.26
  185.8 19.9 %collective-permute-done.16 = bf16[128,2048]{1,0:T(8,128)(2,1)} collective-permute-done((bf16[128,2048]{1,0:T(8,128)(2,1)}, bf16[128,2048]{1,0:T(8,128)(2,1)}, u32[]{:S(2)}, u32[]{:S(2)}) %collective-permute-start.16) | collective-permute-done | bytes 524320 | tf_op jit(solution)/shard_map/ppermute | solution.py:17
  205.7 3.2 %convolution_convert_fusion = bf16[256,2048]{1,0:T(8,128)(2,1)} fusion(bf16[128,2048]{1,0:T(8,128)(2,1)} %collective-permute-done.20, bf16[128,2048]{1,0:T(8,128)(2,1)} %collective-permute-done.19, bf16[128,2048]{1,0:T(8,128)(2,1)} %collective-permute-done.16, bf16[128,2048]{1,0:T(8,128)(2,1)} %get-tuple-element.11, ...), kind=kOutput, calls=%fused_computation.10 | convolution fusion | flops 545914880 | bytes 3276800 | tf_op jit(solution)/shard_map/dot_general | solution.py:12
  209.0 1.3 constant_dynamic-slice_fusion
  210.3 1.9 copy.11
  212.2 2.8 %fusion.35 = bf16[1,512,768]{2,1,0:T(8,128)(2,1)} fusion(bf16[512,768]{1,0:T(8,128)(2,1)} %collective-permute-done.22, f32[2,512,768]{2,1,0:T(8,128)} %copy-done.4, s32[]{:T(128)S(6)} %select_n.107), kind=kLoop, calls=%fused_computation.63 | loop fusion | flops 1179648 | bytes 3145732 | tf_op jit(solution)/shard_map/broadcast_in_dim | solution.py:127
  215.0 2.2 fusion.36
  217.2 13.1 %collective-permute-done.26 = bf16[512,768]{0,1:T(8,128)(2,1)} collective-permute-done((bf16[512,768]{0,1:T(8,128)(2,1)}, bf16[512,768]{0,1:T(8,128)(2,1)}, u32[]{:S(2)}, u32[]{:S(2)}) %collective-permute-start.26) | collective-permute-done | bytes 786464 | tf_op jit(solution)/shard_map/ppermute | solution.py:17
  230.4 2.3 fusion.37
  (90 shorter events, 12.4 us)
Async XLA Ops:
  0.6 8.2 %copy-start = (bf16[256,2048]{1,0:T(8,128)(2,1)S(1)}, bf16[256,2048]{1,0:T(8,128)(2,1)}, u32[]{:S(2)}) copy-start(bf16[256,2048]{1,0:T(8,128)(2,1)} %param.7) | copy-start | bytes 3145732
  0.6 32.9 %collective-permute-start.7 = (bf16[768,512]{1,0:T(8,128)(2,1)}, bf16[768,512]{1,0:T(8,128)(2,1)}, u32[]{:S(2)}, u32[]{:S(2)}) collective-permute-start(bf16[768,512]{1,0:T(8,128)(2,1)} %bitcast.85), channel_id=1, source_target_pairs={{0,1},{1,0},{2,3},{3,2},{4,5},{5,4},{6,7},{7,6},{8,9},{9,8},{10,11... | collective-permute-start | bytes 2359304 | tf_op jit(solution)/shard_map/ppermute | solution.py:22
  1.4 34.9 %collective-permute-start.8 = (bf16[768,512]{1,0:T(8,128)(2,1)}, bf16[768,512]{1,0:T(8,128)(2,1)}, u32[]{:S(2)}, u32[]{:S(2)}) collective-permute-start(bf16[768,512]{1,0:T(8,128)(2,1)} %bitcast.86), channel_id=1, source_target_pairs={{0,2},{1,3},{2,0},{3,1},{4,6},{5,7},{6,4},{7,5},{8,10},{9,11},{10,... | collective-permute-start | bytes 2359304 | tf_op jit(solution)/shard_map/ppermute | solution.py:17
  6.0 4.7 %copy-start.7 = (bf16[256,2048]{1,0:T(8,128)(2,1)S(1)}, bf16[256,2048]{1,0:T(8,128)(2,1)}, u32[]{:S(2)}) copy-start(bf16[256,2048]{1,0:T(8,128)(2,1)} %param.6) | copy-start | bytes 3145732
  7.1 15.2 %collective-permute-start.11 = (bf16[128,2048]{1,0:T(8,128)(2,1)}, bf16[128,2048]{1,0:T(8,128)(2,1)}, u32[]{:S(2)}, u32[]{:S(2)}) collective-permute-start(bf16[128,2048]{1,0:T(8,128)(2,1)} %get-tuple-element.26), channel_id=1, source_target_pairs={{0,4},{4,8},{8,12},{12,0},{1,5},{5,9},{9,13},{13,1},{2,6},{6,10},{... | collective-permute-start | bytes 1572872 | tf_op jit(solution)/shard_map/ppermute | solution.py:17
  8.4 24.6 %collective-permute-start.12 = (bf16[128,2048]{1,0:T(8,128)(2,1)}, bf16[128,2048]{1,0:T(8,128)(2,1)}, u32[]{:S(2)}, u32[]{:S(2)}) collective-permute-start(bf16[128,2048]{1,0:T(8,128)(2,1)} %get-tuple-element.25), channel_id=1, source_target_pairs={{0,12},{4,0},{8,4},{12,8},{1,13},{5,1},{9,5},{13,9},{2,14},{6,2},{... | collective-permute-start | bytes 1572872 | tf_op jit(solution)/shard_map/ppermute | solution.py:17
  8.6 29.1 %collective-permute-start.5 = (bf16[512,768]{1,0:T(8,128)(2,1)}, bf16[512,768]{1,0:T(8,128)(2,1)}, u32[]{:S(2)}, u32[]{:S(2)}) collective-permute-start(bf16[512,768]{1,0:T(8,128)(2,1)} %bitcast.1), channel_id=1, source_target_pairs={{0,2},{1,3},{2,0},{3,1},{4,6},{5,7},{6,4},{7,5},{8,10},{9,11},{10,... | collective-permute-start | bytes 2359304 | tf_op jit(solution)/shard_map/ppermute | solution.py:17
  17.4 1.7 copy-start.8
  20.3 2.0 copy-start.2
  22.3 20.9 %collective-permute-start.4 = (bf16[512,768]{1,0:T(8,128)(2,1)}, bf16[512,768]{1,0:T(8,128)(2,1)}, u32[]{:S(2)}, u32[]{:S(2)}) collective-permute-start(bf16[512,768]{1,0:T(8,128)(2,1)} %bitcast.1), channel_id=1, source_target_pairs={{0,1},{1,0},{2,3},{3,2},{4,5},{5,4},{6,7},{7,6},{8,9},{9,8},{10,11... | collective-permute-start | bytes 2359304 | tf_op jit(solution)/shard_map/ppermute | solution.py:22
  33.0 21.5 %collective-permute-start.2 = (bf16[512,768]{1,0:T(8,128)(2,1)}, bf16[512,768]{1,0:T(8,128)(2,1)}, u32[]{:S(2)}, u32[]{:S(2)}) collective-permute-start(bf16[512,768]{1,0:T(8,128)(2,1)} %bitcast), channel_id=1, source_target_pairs={{0,2},{1,3},{2,0},{3,1},{4,6},{5,7},{6,4},{7,5},{8,10},{9,11},{10,... | collective-permute-start | bytes 2359304 | tf_op jit(solution)/shard_map/ppermute | solution.py:17
  33.5 9.7 %copy-start.15 = (bf16[128,2048]{1,0:T(8,128)(2,1)S(1)}, bf16[128,2048]{1,0:T(8,128)(2,1)}, u32[]{:S(2)}) copy-start(bf16[128,2048]{1,0:T(8,128)(2,1)} %get-tuple-element.18) | copy-start | bytes 1572868
  33.5 21.9 %copy-start.3 = (bf16[2048,768]{1,0:T(8,128)(2,1)S(1)}, bf16[2048,768]{1,0:T(8,128)(2,1)}, u32[]{:S(2)}) copy-start(bf16[2048,768]{1,0:T(8,128)(2,1)} %copy-done.2) | copy-start | bytes 9437188
  33.5 24.3 %collective-permute-start.1 = (bf16[512,768]{1,0:T(8,128)(2,1)}, bf16[512,768]{1,0:T(8,128)(2,1)S(1)}, u32[]{:S(2)}, u32[]{:S(2)}) collective-permute-start(bf16[512,768]{1,0:T(8,128)(2,1)} %bitcast), channel_id=1, source_target_pairs={{0,1},{1,0},{2,3},{3,2},{4,5},{5,4},{6,7},{7,6},{8,9},{9,8},{10,11... | collective-permute-start | bytes 2359304 | tf_op jit(solution)/shard_map/ppermute | solution.py:22
  36.2 21.6 %copy-start.14 = (bf16[128,2048]{1,0:T(8,128)(2,1)S(1)}, bf16[128,2048]{1,0:T(8,128)(2,1)}, u32[]{:S(2)}) copy-start(bf16[128,2048]{1,0:T(8,128)(2,1)} %get-tuple-element.17) | copy-start | bytes 1572868
  36.3 24.2 %collective-permute-start.9 = (bf16[768,512]{1,0:T(8,128)(2,1)}, bf16[768,512]{1,0:T(8,128)(2,1)S(1)}, u32[]{:S(2)}, u32[]{:S(2)}) collective-permute-start(bf16[768,512]{1,0:T(8,128)(2,1)} %collective-permute-done.8), channel_id=1, source_target_pairs={{0,1},{1,0},{2,3},{3,2},{4,5},{5,4},{6,7},{7,6},{8,9},{9,8},{10,11... | collective-permute-start | bytes 2359304 | tf_op jit(solution)/shard_map/ppermute | solution.py:22
  37.7 23.1 %collective-permute-start.6 = (bf16[512,768]{1,0:T(8,128)(2,1)}, bf16[512,768]{1,0:T(8,128)(2,1)S(1)}, u32[]{:S(2)}, u32[]{:S(2)}) collective-permute-start(bf16[512,768]{1,0:T(8,128)(2,1)} %collective-permute-done.5), channel_id=1, source_target_pairs={{0,1},{1,0},{2,3},{3,2},{4,5},{5,4},{6,7},{7,6},{8,9},{9,8},{10,11... | collective-permute-start | bytes 2359304 | tf_op jit(solution)/shard_map/ppermute | solution.py:22
  43.2 17.3 %copy-start.13 = (bf16[128,2048]{1,0:T(8,128)(2,1)S(1)}, bf16[128,2048]{1,0:T(8,128)(2,1)}, u32[]{:S(2)}) copy-start(bf16[128,2048]{1,0:T(8,128)(2,1)} %get-tuple-element.14) | copy-start | bytes 1572868
  43.2 17.4 %copy-start.9 = (bf16[768,2048]{1,0:T(8,128)(2,1)S(1)}, bf16[768,2048]{1,0:T(8,128)(2,1)}, u32[]{:S(2)}) copy-start(bf16[768,2048]{1,0:T(8,128)(2,1)} %constant_dynamic-update-slice_fusion.3) | copy-start | bytes 9437188
  43.2 21.0 %collective-permute-start.18 = (bf16[128,2048]{1,0:T(8,128)(2,1)S(1)}, bf16[128,2048]{1,0:T(8,128)(2,1)S(1)}, u32[]{:S(2)}, u32[]{:S(2)}) collective-permute-start(bf16[128,2048]{1,0:T(8,128)(2,1)S(1)} %copy-done.15), channel_id=1, source_target_pairs={{0,12},{4,0},{8,4},{12,8},{1,13},{5,1},{9,5},{13,9},{2,14},{6,2},{... | collective-permute-start | bytes 1572872 | tf_op jit(solution)/shard_map/ppermute | solution.py:17
  54.5 8.7 %collective-permute-start.3 = (bf16[512,768]{1,0:T(8,128)(2,1)}, bf16[512,768]{1,0:T(8,128)(2,1)S(1)}, u32[]{:S(2)}, u32[]{:S(2)}) collective-permute-start(bf16[512,768]{1,0:T(8,128)(2,1)} %collective-permute-done.2), channel_id=1, source_target_pairs={{0,1},{1,0},{2,3},{3,2},{4,5},{5,4},{6,7},{7,6},{8,9},{9,8},{10,11... | collective-permute-start | bytes 2359304 | tf_op jit(solution)/shard_map/ppermute | solution.py:22
  56.6 4.2 %copy-start.12 = (bf16[128,2048]{1,0:T(8,128)(2,1)S(1)}, bf16[128,2048]{1,0:T(8,128)(2,1)}, u32[]{:S(2)}) copy-start(bf16[128,2048]{1,0:T(8,128)(2,1)} %get-tuple-element.22) | copy-start | bytes 1572868
  57.9 13.7 %collective-permute-start.17 = (bf16[128,2048]{1,0:T(8,128)(2,1)S(1)}, bf16[128,2048]{1,0:T(8,128)(2,1)S(1)}, u32[]{:S(2)}, u32[]{:S(2)}) collective-permute-start(bf16[128,2048]{1,0:T(8,128)(2,1)S(1)} %copy-done.14), channel_id=1, source_target_pairs={{0,4},{4,8},{8,12},{12,0},{1,5},{5,9},{9,13},{13,1},{2,6},{6,10},{... | collective-permute-start | bytes 1572872 | tf_op jit(solution)/shard_map/ppermute | solution.py:17
  60.5 55.1 %collective-permute-start.15 = (bf16[128,2048]{1,0:T(8,128)(2,1)S(1)}, bf16[128,2048]{1,0:T(8,128)(2,1)S(1)}, u32[]{:S(2)}, u32[]{:S(2)}) collective-permute-start(bf16[128,2048]{1,0:T(8,128)(2,1)S(1)} %copy-done.13), channel_id=1, source_target_pairs={{0,8},{4,12},{8,0},{12,4},{1,9},{5,13},{9,1},{13,5},{2,10},{6,14},... | collective-permute-start | bytes 1572872 | tf_op jit(solution)/shard_map/ppermute | solution.py:17
  60.8 66.1 %collective-permute-start = (bf16[128,2048]{1,0:T(8,128)(2,1)S(1)}, bf16[128,2048]{1,0:T(8,128)(2,1)S(1)}, u32[]{:S(2)}, u32[]{:S(2)}) collective-permute-start(bf16[128,2048]{1,0:T(8,128)(2,1)S(1)} %copy-done.12), channel_id=1, source_target_pairs={{0,8},{4,12},{8,0},{12,4},{1,9},{5,13},{9,1},{13,5},{2,10},{6,14},... | collective-permute-start | bytes 1572872 | tf_op jit(solution)/shard_map/ppermute | solution.py:17
  73.8 41.8 %copy-start.10 = (bf16[128,2048]{1,0:T(8,128)(2,1)S(1)}, bf16[128,2048]{1,0:T(8,128)(2,1)}, u32[]{:S(2)}) copy-start(bf16[128,2048]{1,0:T(8,128)(2,1)} %get-tuple-element.13) | copy-start | bytes 1572868
  74.9 51.9 %copy-start.11 = (bf16[128,2048]{1,0:T(8,128)(2,1)S(1)}, bf16[128,2048]{1,0:T(8,128)(2,1)}, u32[]{:S(2)}) copy-start(bf16[128,2048]{1,0:T(8,128)(2,1)} %get-tuple-element.21) | copy-start | bytes 1572868
  74.9 75.2 %collective-permute-start.14 = (bf16[128,2048]{1,0:T(8,128)(2,1)S(1)}, bf16[128,2048]{1,0:T(8,128)(2,1)S(1)}, u32[]{:S(2)}, u32[]{:S(2)}) collective-permute-start(bf16[128,2048]{1,0:T(8,128)(2,1)S(1)} %get-tuple-element.24), channel_id=1, source_target_pairs={{0,4},{4,8},{8,12},{12,0},{1,5},{5,9},{9,13},{13,1},{2,6},{6,10},{... | collective-permute-start | bytes 1572872 | tf_op jit(solution)/shard_map/ppermute | solution.py:17
  76.2 76.3 %collective-permute-start.13 = (bf16[128,2048]{1,0:T(8,128)(2,1)S(1)}, bf16[128,2048]{1,0:T(8,128)(2,1)S(1)}, u32[]{:S(2)}, u32[]{:S(2)}) collective-permute-start(bf16[128,2048]{1,0:T(8,128)(2,1)S(1)} %get-tuple-element.23), channel_id=1, source_target_pairs={{0,12},{4,0},{8,4},{12,8},{1,13},{5,1},{9,5},{13,9},{2,14},{6,2},{... | collective-permute-start | bytes 1572872 | tf_op jit(solution)/shard_map/ppermute | solution.py:17
  130.1 41.7 %collective-permute-start.10 = (bf16[128,2048]{1,0:T(8,128)(2,1)S(1)}, bf16[128,2048]{1,0:T(8,128)(2,1)S(1)}, u32[]{:S(2)}, u32[]{:S(2)}) collective-permute-start(bf16[128,2048]{1,0:T(8,128)(2,1)S(1)} %get-tuple-element.20), channel_id=1, source_target_pairs={{0,8},{4,12},{8,0},{12,4},{1,9},{5,13},{9,1},{13,5},{2,10},{6,14},... | collective-permute-start | bytes 1572872 | tf_op jit(solution)/shard_map/ppermute | solution.py:17
  139.6 33.9 %collective-permute-start.21 = (bf16[2,512,768]{2,1,0:T(8,128)(2,1)S(1)}, bf16[2,512,768]{2,1,0:T(8,128)(2,1)S(1)}, u32[]{:S(2)}, u32[]{:S(2)}) collective-permute-start(bf16[2,512,768]{2,1,0:T(8,128)(2,1)S(1)} %dynamic-slice_bitcast_fusion.2), channel_id=1, source_target_pairs={{0,1},{1,0},{2,3},{3,2},{4,5},{5,4},{6,7},{7,6},{8,9},{9,8},{10,11... | collective-permute-start | bytes 4718600 | tf_op jit(solution)/shard_map/ppermute | solution.py:22
  143.6 34.4 %collective-permute-start.23 = (bf16[2,512,768]{2,1,0:T(8,128)(2,1)S(1)}, bf16[2,512,768]{2,1,0:T(8,128)(2,1)S(1)}, u32[]{:S(2)}, u32[]{:S(2)}) collective-permute-start(bf16[2,512,768]{2,1,0:T(8,128)(2,1)S(1)} %dynamic-slice_bitcast_fusion.1), channel_id=1, source_target_pairs={{0,1},{1,0},{2,3},{3,2},{4,5},{5,4},{6,7},{7,6},{8,9},{9,8},{10,11... | collective-permute-start | bytes 4718600 | tf_op jit(solution)/shard_map/ppermute | solution.py:22
  150.2 30.5 %collective-permute-start.25 = (bf16[2,512,768]{2,1,0:T(8,128)(2,1)S(1)}, bf16[2,512,768]{2,1,0:T(8,128)(2,1)S(1)}, u32[]{:S(2)}, u32[]{:S(2)}) collective-permute-start(bf16[2,512,768]{2,1,0:T(8,128)(2,1)S(1)} %dynamic-slice_bitcast_fusion), channel_id=1, source_target_pairs={{0,1},{1,0},{2,3},{3,2},{4,5},{5,4},{6,7},{7,6},{8,9},{9,8},{10,11... | collective-permute-start | bytes 4718600 | tf_op jit(solution)/shard_map/ppermute | solution.py:22
  152.4 32.4 %collective-permute-start.20 = (bf16[128,2048]{1,0:T(8,128)(2,1)}, bf16[128,2048]{1,0:T(8,128)(2,1)}, u32[]{:S(2)}, u32[]{:S(2)}) collective-permute-start(bf16[128,2048]{1,0:T(8,128)(2,1)} %get-tuple-element.16), channel_id=1, source_target_pairs={{0,4},{4,8},{8,12},{12,0},{1,5},{5,9},{9,13},{13,1},{2,6},{6,10},{... | collective-permute-start | bytes 1572872 | tf_op jit(solution)/shard_map/ppermute | solution.py:17
  171.8 14.1 %collective-permute-start.19 = (bf16[128,2048]{1,0:T(8,128)(2,1)}, bf16[128,2048]{1,0:T(8,128)(2,1)}, u32[]{:S(2)}, u32[]{:S(2)}) collective-permute-start(bf16[128,2048]{1,0:T(8,128)(2,1)} %get-tuple-element.15), channel_id=1, source_target_pairs={{0,12},{4,0},{8,4},{12,8},{1,13},{5,1},{9,5},{13,9},{2,14},{6,2},{... | collective-permute-start | bytes 1572872 | tf_op jit(solution)/shard_map/ppermute | solution.py:17
  173.5 32.2 %collective-permute-start.16 = (bf16[128,2048]{1,0:T(8,128)(2,1)}, bf16[128,2048]{1,0:T(8,128)(2,1)}, u32[]{:S(2)}, u32[]{:S(2)}) collective-permute-start(bf16[128,2048]{1,0:T(8,128)(2,1)} %get-tuple-element.12), channel_id=1, source_target_pairs={{0,8},{4,12},{8,0},{12,4},{1,9},{5,13},{9,1},{13,5},{2,10},{6,14},... | collective-permute-start | bytes 1572872 | tf_op jit(solution)/shard_map/ppermute | solution.py:17
  177.0 2.6 %copy-start.4 = (f32[2,512,768]{2,1,0:T(8,128)}, f32[2,512,768]{2,1,0:T(8,128)S(1)}, u32[]{:S(2)}) copy-start(f32[2,512,768]{2,1,0:T(8,128)S(1)} %convert_add_fusion.2) | copy-start | bytes 9437188
  178.0 34.1 %collective-permute-start.22 = (bf16[512,768]{1,0:T(8,128)(2,1)}, bf16[512,768]{1,0:T(8,128)(2,1)}, u32[]{:S(2)}, u32[]{:S(2)}) collective-permute-start(bf16[512,768]{1,0:T(8,128)(2,1)} %fusion.38), channel_id=1, source_target_pairs={{0,2},{1,3},{2,0},{3,1},{4,6},{5,7},{6,4},{7,5},{8,10},{9,11},{10,... | collective-permute-start | bytes 2359304 | tf_op jit(solution)/shard_map/ppermute | solution.py:17
  179.6 1.9 copy-start.5
  180.7 34.3 %collective-permute-start.24 = (bf16[512,768]{1,0:T(8,128)(2,1)}, bf16[512,768]{1,0:T(8,128)(2,1)}, u32[]{:S(2)}, u32[]{:S(2)}) collective-permute-start(bf16[512,768]{1,0:T(8,128)(2,1)} %fusion.39), channel_id=1, source_target_pairs={{0,2},{1,3},{2,0},{3,1},{4,6},{5,7},{6,4},{7,5},{8,10},{9,11},{10,... | collective-permute-start | bytes 2359304 | tf_op jit(solution)/shard_map/ppermute | solution.py:17
  184.8 45.6 %collective-permute-start.26 = (bf16[512,768]{0,1:T(8,128)(2,1)}, bf16[512,768]{0,1:T(8,128)(2,1)}, u32[]{:S(2)}, u32[]{:S(2)}) collective-permute-start(bf16[512,768]{0,1:T(8,128)(2,1)} %bitcast.87), channel_id=1, source_target_pairs={{0,2},{1,3},{2,0},{3,1},{4,6},{5,7},{6,4},{7,5},{8,10},{9,11},{10,... | collective-permute-start | bytes 2359304 | tf_op jit(solution)/shard_map/ppermute | solution.py:17
  212.1 2.9 %copy-start.6 = (f32[2,512,768]{2,1,0:T(8,128)S(1)}, f32[2,512,768]{2,1,0:T(8,128)}, u32[]{:S(2)}) copy-start(f32[2,512,768]{2,1,0:T(8,128)} %copy-done.5) | copy-start | bytes 9437188
  212.2 20.5 %copy-start.1 = (bf16[256,2048]{1,0:T(8,128)(2,1)S(1)}, bf16[256,2048]{1,0:T(8,128)(2,1)}, u32[]{:S(2)}) copy-start(bf16[256,2048]{1,0:T(8,128)(2,1)} %param.7) | copy-start | bytes 3145732

commit v2 on v1

v2 whole, which is shorter than its diff:
```python
import functools

import jax
import jax.numpy as jnp
from jax import lax
from jax.experimental import pallas as pl
from jax.experimental.pallas import tpu as pltpu
from jax.sharding import PartitionSpec as P

loss_scale = 0.015625
bf16 = jnp.bfloat16
f32 = jnp.float32
MESH = pl.DeviceIdType.MESH
TILE = 256


def dot_dims(left, right, l, r):
    return lax.dot_general(left, right, (((l,), (r,)), ((), ())), preferred_element_type=f32)


def tile_at(i, size):
    return pl.ds(pl.multiple_of(i * size, size), size)


def layer_kernel(
    owners, shards, cap, order,
    sx, sg, wg, wu, wd,
    ho, hg, gate_out, up_out, down_out,
    rx, rg, wgf, wuf, wdf, hid, gg, gu, out, grad, part, from_core, from_x,
    wx_send, wx_recv, wc_send, wc_recv, w_loc,
    in_send, in_recv, in_loc, out_send, out_recv, out_loc,
    rc_send, rc_recv, rx_send, rx_recv,
):
    me = lax.axis_index("expert")
    shard = lax.axis_index("fsdp")
    chips = shards // 2
    chip = shard // 2
    core = lax.rem(shard, 2)
    peer = 2 * chip + 1 - core
    features = rx.shape[1]
    hidden = hid.shape[1]
    size = features // shards
    half = owners // 2
    rows = half * cap

    def at_chip(j):
        return 2 * lax.rem(chip + j, chips) + core

    def remote(src, dst, send, recv, axis, index):
        return pltpu.make_async_remote_copy(
            src_ref=src, dst_ref=dst, send_sem=send, recv_sem=recv,
            device_id={axis: index}, device_id_type=MESH,
        )

    barrier = pltpu.get_barrier_semaphore()
    for k in range(1, owners):
        pl.semaphore_signal(barrier, inc=1, device_id={"expert": lax.rem(me + k, owners)}, device_id_type=MESH)
    for j in range(1, chips):
        pl.semaphore_signal(barrier, inc=1, device_id={"fsdp": at_chip(j)}, device_id_type=MESH)
    pl.semaphore_signal(barrier, inc=1, device_id={"fsdp": peer}, device_id_type=MESH)
    pl.semaphore_wait(barrier, owners - 1 + chips)

    weights = ((wg, wgf, 0), (wu, wuf, 0), (wd, wdf, 1))

    def slab(full, dim, index):
        where = tile_at(index, size)
        return full.at[where, :] if dim == 0 else full.at[:, where]

    over_x, over_core, own = [], [], []
    for w, (src, full, dim) in enumerate(weights):
        over_x.append([
            remote(src, slab(full, dim, shard), wx_send.at[w, j], wx_recv.at[w, j], "fsdp", at_chip(j))
            for j in range(1, chips)
        ])
        first = remote(src, slab(full, dim, shard), wc_send.at[w, 0], wc_recv.at[w, 0], "fsdp", peer)
        over_core.append([first])
        own.append(pltpu.make_async_copy(src, slab(full, dim, shard), w_loc.at[w]))

    def send_in(a, i):
        src, dst = ((sx, rx), (sg, rg))[a]
        where = pl.ds(i * cap, cap)
        if order[i] == 0:
            return pltpu.make_async_copy(src.at[where, :], dst.at[where, :], in_loc.at[a])
        return remote(
            src.at[where, :], dst.at[where, :], in_send.at[a, i], in_recv.at[a, i],
            "expert", lax.rem(me + order[i], owners),
        )

    ins = [[send_in(a, i) for i in range(owners)] for a in range(2)]

    def start_in(c, a):
        for i in range(c * half, (c + 1) * half):
            ins[a][i].start()

    def sent_in(c, a):
        for i in range(c * half, (c + 1) * half):
            if order[i]:
                ins[a][i].wait_send()

    def got_in(c, a):
        for i in range(c * half, (c + 1) * half):
            if order[i]:
                ins[a][i].wait_recv()
            else:
                ins[a][i].wait()

    def forward(w):
        src, full, dim = weights[w]
        for j in range(1, chips):
            over_x[w][j - 1].wait_recv()
            block = slab(full, dim, 2 * lax.rem(chip + chips - j, chips) + core)
            copy = remote(block, block, wc_send.at[w, j], wc_recv.at[w, j], "fsdp", peer)
            copy.start()
            over_core[w].append(copy)

    def got_weight(w):
        own[w].wait()
        for copy in over_core[w]:
            copy.wait_recv()

    for w in range(3):
        for copy in over_x[w]:
            copy.start()
    start_in(0, 0)
    start_in(0, 1)
    for w in range(3):
        over_core[w][0].start()
        own[w].start()
    forward(0)
    sent_in(0, 0)
    start_in(1, 0)
    forward(1)
    sent_in(0, 1)
    start_in(1, 1)
    forward(2)

    def send_out(a, i):
        src, dst = ((out, ho), (grad, hg))[a]
        where = pl.ds(i * cap, cap)
        if order[i] == 0:
            return pltpu.make_async_copy(src.at[where, :], dst.at[where, :], out_loc.at[a])
        return remote(
            src.at[where, :], dst.at[where, :], out_send.at[a, i], out_recv.at[a, i],
            "expert", lax.rem(me + owners - order[i], owners),
        )

    outs = [[send_out(a, i) for i in range(owners)] for a in range(2)]

    def compute(c):
        these = pl.ds(c * rows, rows)
        got_in(c, 0)
        got_in(c, 1)
        if c == 0:
            for w in range(3):
                got_weight(w)

        @pl.loop(0, hidden // TILE)
        def _(t):
            where = tile_at(t, TILE)
            gate_act = jnp.dot(rx[these, :], wgf[:, where], preferred_element_type=f32)
            up_act = jnp.dot(rx[these, :], wuf[:, where], preferred_element_type=f32)
            grad_hidden = dot_dims(rg[these, :], wdf[where, :], 1, 1)
            s = jax.nn.sigmoid(gate_act)
            gated = gate_act * s
            hid[these, where] = (gated * up_act).astype(bf16)
            gg[these, where] = (grad_hidden * up_act * s * (1.0 + gate_act * (1.0 - s))).astype(bf16)
            gu[these, where] = (grad_hidden * gated).astype(bf16)

        @pl.loop(0, features // TILE)
        def _(t):
            where = tile_at(t, TILE)
            out[these, where] = jnp.dot(hid[these, :], wdf[:, where], preferred_element_type=f32).astype(bf16)

        for i in range(c * half, (c + 1) * half):
            outs[0][i].start()

        @pl.loop(0, features // TILE)
        def _(t):
            where = tile_at(t, TILE)
            grad[these, where] = (
                dot_dims(gg[these, :], wgf[where, :], 1, 1) + dot_dims(gu[these, :], wuf[where, :], 1, 1)
            ).astype(bf16)

        for i in range(c * half, (c + 1) * half):
            outs[1][i].start()

    compute(0)
    compute(1)

    def block_partial(index):
        @pl.loop(0, size // TILE)
        def _(t):
            where = pl.ds(pl.multiple_of(index * size + t * TILE, TILE), TILE)
            x = rx[:, where]
            part[where, 0:hidden] = (dot_dims(x, gg[...], 0, 0) * loss_scale).astype(bf16)
            part[where, hidden : 2 * hidden] = (dot_dims(x, gu[...], 0, 0) * loss_scale).astype(bf16)
            part[where, 2 * hidden : 3 * hidden] = (dot_dims(rg[:, where], hid[...], 0, 0) * loss_scale).astype(bf16)

    to_core = []
    for j in range(1, chips + 1):
        slot = j % chips
        index = 2 * lax.rem(chip + j, chips) + 1 - core
        block_partial(index)
        copy = remote(
            part.at[tile_at(index, size), :], from_core.at[slot], rc_send.at[slot], rc_recv.at[slot], "fsdp", peer
        )
        copy.start()
        to_core.append(copy)
    step = 32
    to_x = []
    for j in range(1, chips):
        index = at_chip(j)
        block_partial(index)
        to_core[j - 1].wait_recv()

        @pl.loop(0, size // step)
        def _(t):
            here = pl.ds(pl.multiple_of(index * size + t * step, step), step)
            there = tile_at(t, step)
            part[here, :] = (part[here, :].astype(f32) + from_core[j, there, :].astype(f32)).astype(bf16)

        copy = remote(
            part.at[tile_at(index, size), :], from_x.at[j - 1], rx_send.at[j], rx_recv.at[j], "fsdp", index
        )
        copy.start()
        to_x.append(copy)
    block_partial(shard)
    to_core[chips - 1].wait_recv()
    for copy in to_x:
        copy.wait_recv()

    @pl.loop(0, size // step)
    def _(t):
        here = pl.ds(pl.multiple_of(shard * size + t * step, step), step)
        there = tile_at(t, step)
        total = part[here, :].astype(f32) + from_core[0, there, :].astype(f32)
        for j in range(1, chips):
            total = total + from_x[j - 1, there, :].astype(f32)
        total = total.astype(bf16)
        gate_out[there, :] = total[:, 0:hidden]
        up_out[there, :] = total[:, hidden : 2 * hidden]
        down_out[there, :] = total[:, 2 * hidden : 3 * hidden]

    for w in range(3):
        for copy in over_x[w] + over_core[w]:
            copy.wait_send()
    for a in range(2):
        sent_in(1, a)
    for copy in to_core + to_x:
        copy.wait_send()
    for a in range(2):
        for copy in outs[a]:
            copy.wait()


def body(tokens, cotangent, expert_ids, gate_weight, up_weight, down_weight):
    rows, features = tokens.shape
    hidden = gate_weight.shape[2]
    owners = lax.axis_size("expert")
    shards = lax.axis_size("fsdp")
    chips = shards // 2
    me = lax.axis_index("expert")
    cap = 2 * rows // owners
    slots = owners * cap
    size = features // shards
    order = [k for k in range(owners) if k % 2 == 0] + [k for k in range(owners) if k % 2]
    onehot = (expert_ids[:, None] == jnp.arange(owners, dtype=jnp.int32)[None, :]).astype(bf16)
    t = jnp.arange(rows, dtype=jnp.int32)
    before = (t[None, :] < t[:, None]).astype(bf16)
    earlier = jnp.dot(before, onehot, preferred_element_type=f32)
    rank = jnp.sum(earlier * onehot.astype(f32), axis=1).astype(jnp.int32)
    k = (expert_ids - me + owners) % owners
    place = k // 2 + (k % 2) * (owners // 2)
    slot = place * cap + rank
    pick = (jnp.arange(slots, dtype=jnp.int32)[:, None] == slot[None, :]).astype(bf16)
    sx = jnp.dot(pick, tokens, preferred_element_type=f32).astype(bf16)
    sg = jnp.dot(pick, cotangent, preferred_element_type=f32).astype(bf16)

    dma = pltpu.SemaphoreType.DMA
    anywhere = pl.BlockSpec(memory_space=pl.ANY)
    vmem = pl.BlockSpec(memory_space=pltpu.VMEM)
    row_shape = jax.ShapeDtypeStruct((slots, features), bf16)
    sum_shape = jax.ShapeDtypeStruct((size, hidden), bf16)
    ho, hg, gate_grad, up_grad, down_grad = pl.pallas_call(
        functools.partial(layer_kernel, owners, shards, cap, order),
        out_shape=(row_shape, row_shape, sum_shape, sum_shape, sum_shape),
        in_specs=[anywhere] * 5,
        out_specs=(anywhere, anywhere, vmem, vmem, vmem),
        scratch_shapes=[
            pltpu.VMEM((slots, features), bf16),
            pltpu.VMEM((slots, features), bf16),
            pltpu.VMEM((features, hidden), bf16),
            pltpu.VMEM((features, hidden), bf16),
            pltpu.VMEM((hidden, features), bf16),
            pltpu.VMEM((slots, hidden), bf16),
            pltpu.VMEM((slots, hidden), bf16),
            pltpu.VMEM((slots, hidden), bf16),
            pltpu.VMEM((slots, features), bf16),
            pltpu.VMEM((slots, features), bf16),
            pltpu.VMEM((features, 3 * hidden), bf16),
            pltpu.VMEM((chips, size, 3 * hidden), bf16),
            pltpu.VMEM((chips - 1, size, 3 * hidden), bf16),
            dma((3, chips)), dma((3, chips)), dma((3, chips)), dma((3, chips)), dma((3,)),
            dma((2, owners)), dma((2, owners)), dma((2,)),
            dma((2, owners)), dma((2, owners)), dma((2,)),
            dma((chips,)), dma((chips,)), dma((chips,)), dma((chips,)),
        ],
        compiler_params=pltpu.CompilerParams(
            collective_id=0, has_side_effects=True, vmem_limit_bytes=58 * 1024 * 1024
        ),
        cost_estimate=pl.CostEstimate(
            flops=18 * slots * features * hidden, bytes_accessed=40 * 1024 * 1024, transcendentals=slots * hidden
        ),
    )(sx, sg, gate_weight[0], up_weight[0], down_weight[0])
    layer_output = dot_dims(pick, ho, 0, 0).astype(bf16)
    grad_tokens = dot_dims(pick, hg, 0, 0).astype(bf16)
    return (layer_output, grad_tokens, gate_grad[None], up_grad[None], jnp.transpose(down_grad)[None])


def solution(mesh):
    rows = P(("groups", "expert", "fsdp"), None)
    return jax.shard_map(
        body,
        mesh=mesh,
        in_specs=(
            rows,
            rows,
            P(("groups", "expert", "fsdp")),
            P("expert", "fsdp", None),
            P("expert", "fsdp", None),
            P("expert", None, "fsdp"),
        ),
        out_specs=(
            rows,
            rows,
            P(("groups", "expert"), "fsdp", None),
            P(("groups", "expert"), "fsdp", None),
            P(("groups", "expert"), None, "fsdp"),
        ),
        check_vma=False,
    )
```

time: 236 us -> 225 us (0.953); the launches traced: 233 us -> 225 us
  Pallas kernels: 0 us -> 211 us
  waiting for transfers between devices: 123 us -> 0 us
  starting transfers between devices: 34.1 us -> 0 us
  local copies, waits for them, and re-layouts: 33.9 us -> 2.95 us
  matrix products: 30.6 us -> 10.3 us
  other arithmetic: 9.24 us -> 0.71 us
    pallas_call x0 -> x1, Pallas kernels: none -> 211 us  [body(): pl.pallas_call(functools.partial(layer_kernel, owners, shards, cap, order...]
    ppermute x27 -> x0, waiting for transfers between devices: 123 us -> none  [the longest x18 123 us: shift(): return lax.ppermute(x, axis, [(i, (i + k) % n) for i in range(n)])]
    ppermute x27 -> x0, starting transfers between devices: 34.1 us -> none  [the longest x18 17.7 us: shift(): return lax.ppermute(x, axis, [(i, (i + k) % n) for i in range(n)])]
    dot_general x11 -> x2, matrix products: 19.2 us -> 5.2 us  [dot_dims(): lax.dot_general(left, right, (((l,), (r,)), ((), ())), preferred_element_...]
    dynamic_update_slice x12 -> x0, local copies, waits for them, and re-layouts: 12.4 us -> none  [the longest x6 8.77 us: gather_weight(): full = lax.dynamic_update_slice_in_dim(full, mine, owner * size, dim)]
    slice x8 -> x0, local copies, waits for them, and re-layouts: 7.91 us -> none  [the longest x4 5.58 us: body(): sent[i * cap:(i + 1) * cap]]
    broadcast_in_dim x3 -> x0, other arithmetic: 7.32 us -> none  [the longest x1 2.84 us: body(): gate_grad = scatter_sum(gate_part)[None]]
    dot_general x10 -> x2, matrix products: 10.4 us -> 4.07 us  [the longest x1 2.05 us: body(): sx = jnp.dot(pick, tokens, preferred_element_type=f32).astype(bf16)]
  transfers between devices with their start and end apart: 27 -> 0, of which waited for: 9 -> 0; matrix products, arithmetic and copies ran while one was open for 30% -> 0% of each run, Pallas kernels for 0% -> 0%
where the time goes in v2:
time: 225 us
  Pallas kernels  211 us (94%)
  matrix products  10.3 us (5%)
  local copies, waits for them, and re-layouts  2.95 us (1%)
    pallas_call x1, Pallas kernels, body(): pl.pallas_call(functools.partial(layer_kernel, owners, shards, cap, order...  211 us
    dot_general x2, matrix products, dot_dims(): lax.dot_general(left, right, (((l,), (r,)), ((), ())), preferred_element_...  5.2 us

profile of v2, /device:TPU:21, one launch (start us, length us, event | category | flops | bytes accessed | tf_op | source)
XLA Modules:
  0.0 225.2 jit_solution(15216764785473407490)
XLA Ops:
  0.6 0.0 copy-start
  0.6 0.0 copy-start.2
  0.7 1.0 fusion
  1.7 0.7 convert_add_fusion
  2.4 0.0 copy-done
  2.4 2.0 convolution_convert_fusion.sg
  4.4 0.0 copy-done.2
  4.4 2.0 convolution_convert_fusion.1.sx
  6.5 210.5 %shard_map.101 = (bf16[512,2048]{1,0:T(8,128)(2,1)}, bf16[512,2048]{1,0:T(8,128)(2,1)}, bf16[512,768]{1,0:T(8,128)(2,1)}, bf16[512,768]{1,0:T(8,128)(2,1)}, bf16[512,768]{1,0:T(8,128)(2,1)}) custom-call(bf16[512,2048]{1,0:T(8,128)(2,1)} %convolution_convert_fusion.1.sx, bf16[512,2048]{1,0:T(8,128)(2,1)} %convolution_convert_fusion.sg, ...), custom_call_target="tpu_custom_call" | custom-call | flops 14495514624 | bytes 41943040 | tf_op jit(solution)/shard_map/pallas_call | solution.py:284
  217.0 0.0 copy-start.1
  217.0 3.5 %convolution_convert_fusion.3 = bf16[256,2048]{1,0:T(8,128)(2,1)} fusion(bf16[512,2048]{1,0:T(8,128)(2,1)} %get-tuple-element.10, s32[256]{0:T(256)S(1)} %convert_add_fusion), kind=kOutput, calls=%fused_computation.3 | convolution fusion | flops 537526272 | bytes 3146752 | tf_op jit(solution)/shard_map/dot_general | solution.py:18
  220.5 0.0 copy-done.1
  220.5 0.0 copy-start.5
  220.5 0.0 copy-start.4
  220.5 1.7 convolution_convert_fusion.2
  222.3 0.0 copy-done.5
  222.3 0.0 copy-start.3
  222.3 1.2 copy.11
  223.4 0.0 copy-done.4
  223.4 0.9 copy.14
  224.3 0.0 copy-done.3
  224.3 0.9 copy.15
Async XLA Ops:
  0.6 1.8 copy-start
  0.6 3.8 %copy-start.2 = (bf16[256,2048]{1,0:T(8,128)(2,1)S(1)}, bf16[256,2048]{1,0:T(8,128)(2,1)}, u32[]{:S(2)}) copy-start(bf16[256,2048]{1,0:T(8,128)(2,1)} %param.6) | copy-start | bytes 3145732
  217.0 3.5 %copy-start.1 = (bf16[512,2048]{1,0:T(8,128)(2,1)S(1)}, bf16[512,2048]{1,0:T(8,128)(2,1)}, u32[]{:S(2)}) copy-start(bf16[512,2048]{1,0:T(8,128)(2,1)} %get-tuple-element.11) | copy-start | bytes 6291460
  220.5 1.7 copy-start.5
  220.5 2.9 %copy-start.4 = (bf16[512,768]{1,0:T(8,128)(2,1)S(1)}, bf16[512,768]{1,0:T(8,128)(2,1)}, u32[]{:S(2)}) copy-start(bf16[512,768]{1,0:T(8,128)(2,1)} %get-tuple-element.12) | copy-start | bytes 2359300
  222.3 2.0 copy-start.3

commit v3 on v2

--- a/solution.py
+++ b/solution.py
@@ -24,11 +24,11 @@
 
 def layer_kernel(
     owners, shards, cap, order,
-    sx, sg, wg, wu, wd,
+    pick, tok, cot, wg, wu, wd,
     ho, hg, gate_out, up_out, down_out,
-    rx, rg, wgf, wuf, wdf, hid, gg, gu, out, grad, part, from_core, from_x,
+    sx, sg, rx, rg, wgf, wuf, wdf, hid, gg, gu, out, grad, part, from_core, from_x,
     wx_send, wx_recv, wc_send, wc_recv, w_loc,
-    in_send, in_recv, in_loc, out_send, out_recv, out_loc,
+    in_send, in_recv, out_send, out_recv, out_loc,
     rc_send, rc_recv, rx_send, rx_recv,
 ):
     me = lax.axis_index("expert")
@@ -80,7 +80,7 @@
         src, dst = ((sx, rx), (sg, rg))[a]
         where = pl.ds(i * cap, cap)
         if order[i] == 0:
-            return pltpu.make_async_copy(src.at[where, :], dst.at[where, :], in_loc.at[a])
+            return None
         return remote(
             src.at[where, :], dst.at[where, :], in_send.at[a, i], in_recv.at[a, i],
             "expert", lax.rem(me + order[i], owners),
@@ -89,8 +89,21 @@
     ins = [[send_in(a, i) for i in range(owners)] for a in range(2)]
 
     def start_in(c, a):
+        rows_in, sent, kept = ((tok, sx, rx), (cot, sg, rg))[a]
+        low = cap if c == 0 else 0
+        picked = pick[c * rows : (c + 1) * rows, :]
+
+        @pl.loop(0, features // TILE)
+        def _(t):
+            where = tile_at(t, TILE)
+            block = jnp.dot(picked, rows_in[:, where], preferred_element_type=f32).astype(bf16)
+            if c == 0:
+                kept[0:cap, where] = block[0:cap]
+            sent[c * rows + low : (c + 1) * rows, where] = block[low:]
+
         for i in range(c * half, (c + 1) * half):
-            ins[a][i].start()
+            if order[i]:
+                ins[a][i].start()
 
     def sent_in(c, a):
         for i in range(c * half, (c + 1) * half):
@@ -101,8 +114,6 @@
         for i in range(c * half, (c + 1) * half):
             if order[i]:
                 ins[a][i].wait_recv()
-            else:
-                ins[a][i].wait()
 
     def forward(w):
         src, full, dim = weights[w]
@@ -146,14 +157,12 @@
 
     outs = [[send_out(a, i) for i in range(owners)] for a in range(2)]
 
+    def start_out(c, a):
+        for i in range(c * half, (c + 1) * half):
+            outs[a][i].start()
+
     def compute(c):
         these = pl.ds(c * rows, rows)
-        got_in(c, 0)
-        got_in(c, 1)
-        if c == 0:
-            for w in range(3):
-                got_weight(w)
-
         @pl.loop(0, hidden // TILE)
         def _(t):
             where = tile_at(t, TILE)
@@ -171,8 +180,8 @@
             where = tile_at(t, TILE)
             out[these, where] = jnp.dot(hid[these, :], wdf[:, where], preferred_element_type=f32).astype(bf16)
 
-        for i in range(c * half, (c + 1) * half):
-            outs[0][i].start()
+        if c == 1:
+            start_out(c, 0)
 
         @pl.loop(0, features // TILE)
         def _(t):
@@ -181,10 +190,18 @@
                 dot_dims(gg[these, :], wgf[where, :], 1, 1) + dot_dims(gu[these, :], wuf[where, :], 1, 1)
             ).astype(bf16)
 
-        for i in range(c * half, (c + 1) * half):
-            outs[1][i].start()
-
+        if c == 1:
+            start_out(c, 1)
+
+    got_in(0, 0)
+    got_in(0, 1)
+    for w in range(3):
+        got_weight(w)
     compute(0)
+    got_in(1, 0)
+    start_out(0, 0)
+    got_in(1, 1)
+    start_out(0, 1)
     compute(1)
 
     def block_partial(index):
@@ -273,8 +290,6 @@
     place = k // 2 + (k % 2) * (owners // 2)
     slot = place * cap + rank
     pick = (jnp.arange(slots, dtype=jnp.int32)[:, None] == slot[None, :]).astype(bf16)
-    sx = jnp.dot(pick, tokens, preferred_element_type=f32).astype(bf16)
-    sg = jnp.dot(pick, cotangent, preferred_element_type=f32).astype(bf16)
 
     dma = pltpu.SemaphoreType.DMA
     anywhere = pl.BlockSpec(memory_space=pl.ANY)
@@ -284,9 +299,11 @@
     ho, hg, gate_grad, up_grad, down_grad = pl.pallas_call(
         functools.partial(layer_kernel, owners, shards, cap, order),
         out_shape=(row_shape, row_shape, sum_shape, sum_shape, sum_shape),
-        in_specs=[anywhere] * 5,
+        in_specs=[vmem] * 3 + [anywhere] * 3,
         out_specs=(anywhere, anywhere, vmem, vmem, vmem),
         scratch_shapes=[
+            pltpu.VMEM((slots, features), bf16),
+            pltpu.VMEM((slots, features), bf16),
             pltpu.VMEM((slots, features), bf16),
             pltpu.VMEM((slots, features), bf16),
             pltpu.VMEM((features, hidden), bf16),
@@ -301,7 +318,7 @@
             pltpu.VMEM((chips, size, 3 * hidden), bf16),
             pltpu.VMEM((chips - 1, size, 3 * hidden), bf16),
             dma((3, chips)), dma((3, chips)), dma((3, chips)), dma((3, chips)), dma((3,)),
-            dma((2, owners)), dma((2, owners)), dma((2,)),
+            dma((2, owners)), dma((2, owners)),
             dma((2, owners)), dma((2, owners)), dma((2,)),
             dma((chips,)), dma((chips,)), dma((chips,)), dma((chips,)),
         ],
@@ -311,7 +328,7 @@
         cost_estimate=pl.CostEstimate(
             flops=18 * slots * features * hidden, bytes_accessed=40 * 1024 * 1024, transcendentals=slots * hidden
         ),
-    )(sx, sg, gate_weight[0], up_weight[0], down_weight[0])
+    )(pick, tokens, cotangent, gate_weight[0], up_weight[0], down_weight[0])
     layer_output = dot_dims(pick, ho, 0, 0).astype(bf16)
     grad_tokens = dot_dims(pick, hg, 0, 0).astype(bf16)
     return (layer_output, grad_tokens, gate_grad[None], up_grad[None], jnp.transpose(down_grad)[None])

time: 225 us -> 214 us (0.951)
  Pallas kernels: 211 us -> 202 us
  matrix products: 10.3 us -> 6.15 us
    pallas_call x1, Pallas kernels: 211 us -> 202 us  [body(): pl.pallas_call(functools.partial(layer_kernel, owners, shards, cap, order...]
    dot_general x2 -> x0, matrix products: 4.07 us -> none  [the longest x1 2.05 us: body(): sx = jnp.dot(pick, tokens, preferred_element_type=f32).astype(bf16)]
where the time goes in v3:
time: 214 us; the launch traced here: 213 us
  Pallas kernels  202 us (94%)
  matrix products  6.15 us (3%)
  local copies, waits for them, and re-layouts  2.93 us (1%)
    pallas_call x1, Pallas kernels, body(): pl.pallas_call(functools.partial(layer_kernel, owners, shards, cap, order...  202 us
    dot_general x2, matrix products, dot_dims(): lax.dot_general(left, right, (((l,), (r,)), ((), ())), preferred_element_...  5.2 us

profile of v3, /device:TPU:21, one launch (start us, length us, event | category | flops | bytes accessed | tf_op | source)
XLA Modules:
  0.0 213.4 jit_solution(991261097236148673)
XLA Ops:
  0.6 1.0 fusion
  1.6 0.7 convert_add_fusion
  2.3 0.8 fusion.1.pick
  3.1 202.2 %shard_map.101 = (bf16[512,2048]{1,0:T(8,128)(2,1)}, bf16[512,2048]{1,0:T(8,128)(2,1)}, bf16[512,768]{1,0:T(8,128)(2,1)}, bf16[512,768]{1,0:T(8,128)(2,1)}, bf16[512,768]{1,0:T(8,128)(2,1)}) custom-call(bf16[512,256]{1,0:T(8,128)(2,1)} %fusion.1.pick, bf16[256,2048]{1,0:T(8,128)(2,1)} %tok.1, bf16[256,2048]{1,0:T(8,128)(2,1)} %cot.1, ...), custom_call_target="tpu_custom_call" | custom-call | flops 14495514624 | bytes 41943040 | tf_op jit(solution)/shard_map/pallas_call | solution.py:299
  205.3 0.0 copy-start
  205.3 3.5 %convolution_convert_fusion.1 = bf16[256,2048]{1,0:T(8,128)(2,1)} fusion(bf16[512,2048]{1,0:T(8,128)(2,1)} %get-tuple-element.10, s32[256]{0:T(256)S(1)} %convert_add_fusion), kind=kOutput, calls=%fused_computation.1 | convolution fusion | flops 537526272 | bytes 3146752 | tf_op jit(solution)/shard_map/dot_general | solution.py:18
  208.7 0.0 copy-done
  208.7 0.0 copy-start.3
  208.7 0.0 copy-start.2
  208.7 1.7 convolution_convert_fusion
  210.5 0.0 copy-done.3
  210.5 0.0 copy-start.1
  210.5 1.2 copy.11
  211.6 0.0 copy-done.2
  211.6 0.9 copy.14
  212.5 0.0 copy-done.1
  212.5 0.9 copy.15
Async XLA Ops:
  205.3 3.5 %copy-start = (bf16[512,2048]{1,0:T(8,128)(2,1)S(1)}, bf16[512,2048]{1,0:T(8,128)(2,1)}, u32[]{:S(2)}) copy-start(bf16[512,2048]{1,0:T(8,128)(2,1)} %get-tuple-element.11) | copy-start | bytes 6291460
  208.7 1.7 copy-start.3
  208.7 2.9 %copy-start.2 = (bf16[512,768]{1,0:T(8,128)(2,1)S(1)}, bf16[512,768]{1,0:T(8,128)(2,1)}, u32[]{:S(2)}) copy-start(bf16[512,768]{1,0:T(8,128)(2,1)} %get-tuple-element.12) | copy-start | bytes 2359300
  210.5 2.0 copy-start.1

commit v4 on v3

--- a/solution.py
+++ b/solution.py
@@ -88,6 +88,19 @@
 
     ins = [[send_in(a, i) for i in range(owners)] for a in range(2)]
 
+    def start_far_first(copies, c, flip):
+        mine = [copy for copy in copies[c * half : (c + 1) * half] if copy is not None]
+
+        @pl.when(lax.rem(me + flip, 2) == 0)
+        def _():
+            for copy in mine:
+                copy.start()
+
+        @pl.when(lax.rem(me + flip, 2) == 1)
+        def _():
+            for copy in reversed(mine):
+                copy.start()
+
     def start_in(c, a):
         rows_in, sent, kept = ((tok, sx, rx), (cot, sg, rg))[a]
         low = cap if c == 0 else 0
@@ -101,9 +114,7 @@
                 kept[0:cap, where] = block[0:cap]
             sent[c * rows + low : (c + 1) * rows, where] = block[low:]
 
-        for i in range(c * half, (c + 1) * half):
-            if order[i]:
-                ins[a][i].start()
+        start_far_first(ins[a], c, 1)
 
     def sent_in(c, a):
         for i in range(c * half, (c + 1) * half):
@@ -158,8 +169,7 @@
     outs = [[send_out(a, i) for i in range(owners)] for a in range(2)]
 
     def start_out(c, a):
-        for i in range(c * half, (c + 1) * half):
-            outs[a][i].start()
+        start_far_first(outs[a], c, 0)
 
     def compute(c):
         these = pl.ds(c * rows, rows)

time: 214 us -> 214 us (level)
  no operation moved by 1% of the time
where the time goes in v4:
time: 214 us; the launch traced here: 213 us
  Pallas kernels  202 us (94%)
  matrix products  6.15 us (3%)
  local copies, waits for them, and re-layouts  2.93 us (1%)
    pallas_call x1, Pallas kernels, body(): pl.pallas_call(functools.partial(layer_kernel, owners, shards, cap, order...  202 us
    dot_general x2, matrix products, dot_dims(): lax.dot_general(left, right, (((l,), (r,)), ((), ())), preferred_element_...  5.2 us

profile of v4, /device:TPU:21, one launch (start us, length us, event | category | flops | bytes accessed | tf_op | source)
XLA Modules:
  0.0 213.5 jit_solution(5888568574174242189)
XLA Ops:
  0.6 1.0 fusion
  1.6 0.7 convert_add_fusion
  2.3 0.8 fusion.1.pick
  3.1 202.3 %shard_map.101 = (bf16[512,2048]{1,0:T(8,128)(2,1)}, bf16[512,2048]{1,0:T(8,128)(2,1)}, bf16[512,768]{1,0:T(8,128)(2,1)}, bf16[512,768]{1,0:T(8,128)(2,1)}, bf16[512,768]{1,0:T(8,128)(2,1)}) custom-call(bf16[512,256]{1,0:T(8,128)(2,1)} %fusion.1.pick, bf16[256,2048]{1,0:T(8,128)(2,1)} %tok.1, bf16[256,2048]{1,0:T(8,128)(2,1)} %cot.1, ...), custom_call_target="tpu_custom_call" | custom-call | flops 14495514624 | bytes 41943040 | tf_op jit(solution)/shard_map/pallas_call | solution.py:309
  205.3 0.0 copy-start
  205.4 3.5 %convolution_convert_fusion.1 = bf16[256,2048]{1,0:T(8,128)(2,1)} fusion(bf16[512,2048]{1,0:T(8,128)(2,1)} %get-tuple-element.10, s32[256]{0:T(256)S(1)} %convert_add_fusion), kind=kOutput, calls=%fused_computation.1 | convolution fusion | flops 537526272 | bytes 3146752 | tf_op jit(solution)/shard_map/dot_general | solution.py:18
  208.8 0.0 copy-done
  208.8 0.0 copy-start.3
  208.8 0.0 copy-start.2
  208.8 1.7 convolution_convert_fusion
  210.6 0.0 copy-done.3
  210.6 0.0 copy-start.1
  210.6 1.2 copy.11
  211.7 0.0 copy-done.2
  211.7 0.9 copy.14
  212.6 0.0 copy-done.1
  212.6 0.9 copy.15
Async XLA Ops:
  205.3 3.5 %copy-start = (bf16[512,2048]{1,0:T(8,128)(2,1)S(1)}, bf16[512,2048]{1,0:T(8,128)(2,1)}, u32[]{:S(2)}) copy-start(bf16[512,2048]{1,0:T(8,128)(2,1)} %get-tuple-element.11) | copy-start | bytes 6291460
  208.8 1.7 copy-start.3
  208.8 2.9 %copy-start.2 = (bf16[512,768]{1,0:T(8,128)(2,1)S(1)}, bf16[512,768]{1,0:T(8,128)(2,1)}, u32[]{:S(2)}) copy-start(bf16[512,768]{1,0:T(8,128)(2,1)} %get-tuple-element.12) | copy-start | bytes 2359300
  210.6 2.0 copy-start.1
